TPU v7x, 32 devices: a whole 2x2x4 slice. The times are simulated.
32 devices in a mesh: ep: 16 (over z, y, x), dp: 2 (over core).
Axes of the slice: x: 2, y: 2, z: 4, core: 2. Of those that a mesh axis runs over, the one named last changes fastest.
Arguments:
- attention_out: bfloat16 [2048, 2560], P(('ep', 'dp')), may hold values from -6 to 6
- residual: bfloat16 [2048, 2560], P(('ep', 'dp')), may hold values from -30 to 30
- out_weight: bfloat16 [2560, 2560], P(None, 'dp'), may hold values from -0.125 to 0.125
- pre_gain: float32 [2560], replicated, may hold values from 0.5 to 1.5
- routes: int32 [2048, 6], P(('ep', 'dp')), may hold values from 0 to 15, all different within a row; in each aligned block of 64 rows (0 to 63, 64 to 127, ...) at most 36 rows name the same one
- gate_prob: float32 [2048, 6], P(('ep', 'dp')), may hold values from 0.05 to 1
- gate_weight: bfloat16 [16, 2560, 1536], P('ep', None, 'dp'), may hold values from -0.125 to 0.125
- up_weight: bfloat16 [16, 2560, 1536], P('ep', None, 'dp'), may hold values from -0.125 to 0.125
- down_weight: bfloat16 [16, 1536, 2560], P('ep', None, 'dp'), may hold values from -0.15625 to 0.15625
- post_gain: float32 [2560], replicated, may hold values from 0.5 to 1.5
Outputs:
- new_state: bfloat16 [2048, 2560], P(('ep', 'dp'))
- normed_state: bfloat16 [2048, 2560], P(('ep', 'dp'))
Inputs may be any that keep to these rules, and one draw needn't show every extreme that they name: `routes`: each row names 6 different experts; within the 64 rows of one device no expert is named more than 36 times, a bound that some block reaches.
All inputs are finite; a program needn't handle non-finite values.
Results may differ from a plain program's by a relative error of at most 0.015.
Values may be sent and summed in bfloat16 or wider, within the bound.
A program may use at most 128 MiB of HBM per device.

v0:
```python
import jax
import jax.numpy as jnp
from jax import lax
from jax.sharding import PartitionSpec as P


def rms_scale(values, gain):
    widened = values.astype(jnp.float32)
    meansq = jnp.mean(widened * widened, axis=-1, keepdims=True)
    return widened * lax.rsqrt(meansq + 1e-06) * gain


def slot_table(route_block, experts, capacity):
    flat_ids = route_block.reshape(-1)
    onehot = (flat_ids[:, None] == jnp.arange(experts, dtype=jnp.int32)[None, :]).astype(jnp.int32)
    before = jnp.cumsum(onehot, axis=0) - onehot
    rank_in = jnp.sum(before * onehot, axis=1)
    return (flat_ids * capacity + rank_in).reshape(route_block.shape)


def per_device(
    attention_out,
    residual,
    out_weight,
    pre_gain,
    routes,
    gate_prob,
    gate_weight,
    up_weight,
    down_weight,
    post_gain,
):
    groups = lax.axis_size("dp")
    experts = lax.axis_size("ep")
    tok_rows, top_picks = routes.shape
    row_width = residual.shape[1]
    part_cols = out_weight.shape[1]
    capacity = max(2, 3 * tok_rows * top_picks // (2 * experts))
    columns = jnp.dot(
        lax.all_gather(attention_out, "dp", axis=0, tiled=True),
        out_weight,
        preferred_element_type=jnp.float32,
    )
    home_cols = lax.all_to_all(
        columns.reshape(groups, tok_rows, part_cols).astype(jnp.bfloat16),
        "dp",
        split_axis=0,
        concat_axis=2,
        tiled=True,
    ).astype(jnp.float32)
    summed = (residual.astype(jnp.float32) + home_cols.reshape(tok_rows, row_width)).astype(
        jnp.bfloat16
    )
    normed_in = rms_scale(summed, pre_gain).astype(jnp.bfloat16)
    slot_ids = slot_table(routes, experts, capacity)
    matches = (
        slot_ids[:, :, None] == jnp.arange(experts * capacity, dtype=jnp.int32)[None, None, :]
    ).astype(jnp.float32)
    placing = jnp.sum(matches, axis=1).astype(jnp.bfloat16)
    weights = gate_prob / jnp.sum(gate_prob, axis=1, keepdims=True)
    mixing = jnp.sum(weights[:, :, None] * matches, axis=1)
    outgoing = lax.dot_general(
        placing, normed_in, (((0,), (0,)), ((), ())), preferred_element_type=jnp.float32
    ).astype(jnp.bfloat16)
    gate_local = gate_weight[0]
    up_local = up_weight[0]
    down_local = down_weight[0]
    arrived = lax.all_to_all(
        outgoing.reshape(experts, capacity, row_width),
        "ep",
        split_axis=0,
        concat_axis=0,
        tiled=True,
    )
    segment = lax.all_gather(arrived.reshape(-1, row_width), "dp", axis=0, tiled=True)
    gate_part = jnp.dot(segment, gate_local, preferred_element_type=jnp.float32)
    up_part = jnp.dot(segment, up_local, preferred_element_type=jnp.float32)
    hidden = (jax.nn.silu(gate_part) * up_part).astype(jnp.bfloat16)
    results = jnp.dot(
        lax.all_gather(hidden, "dp", axis=1, tiled=True),
        down_local,
        preferred_element_type=jnp.float32,
    ).astype(jnp.bfloat16)
    joined = lax.all_to_all(
        results.reshape(groups, experts * capacity, part_cols),
        "dp",
        split_axis=0,
        concat_axis=2,
        tiled=True,
    )
    returned_rows = lax.all_to_all(
        joined.reshape(experts, capacity, row_width), "ep", split_axis=0, concat_axis=0, tiled=True
    )
    returned = returned_rows.reshape(experts * capacity, row_width).astype(jnp.float32)
    expert_sum = jnp.dot(
        mixing, returned, precision=lax.Precision.HIGHEST, preferred_element_type=jnp.float32
    )
    new_state = (summed.astype(jnp.float32) + expert_sum).astype(jnp.bfloat16)
    normed_state = rms_scale(new_state, post_gain).astype(jnp.bfloat16)
    return (new_state, normed_state)


def solution(mesh):
    return jax.shard_map(
        per_device,
        mesh=mesh,
        in_specs=(
            P(("ep", "dp"), None),
            P(("ep", "dp"), None),
            P(None, "dp"),
            P(),
            P(("ep", "dp"), None),
            P(("ep", "dp"), None),
            P("ep", None, "dp"),
            P("ep", None, "dp"),
            P("ep", None, "dp"),
            P(),
        ),
        out_specs=(P(("ep", "dp"), None), P(("ep", "dp"), None)),
        check_vma=False,
    )
```

profile of v0, /device:TPU:0, one launch (start us, length us, event | category | flops | bytes accessed | tf_op | source)
XLA Modules:
  0.0 276.7 jit_solution(12917749217615015285)
XLA Ops:
  7.2 2.6 all_gather.9
  9.7 4.6 %convolution_convert_fusion.2 = bf16[128,1280]{1,0:T(8,128)(2,1)} fusion(bf16[128,2560]{1,0:T(8,128)(2,1)S(1)} %all_gather.9, bf16[2560,1280]{1,0:T(8,128)(2,1)} %param.12), kind=kOutput, calls=%fused_computation.10 | convolution fusion | flops 839024640 | bytes 7536640 | tf_op jit(solution)/shard_map/dot_general | solution.py:39
  14.4 3.6 %all-to-all-start = ((bf16[2,64,1280]{2,1,0:T(8,128)(2,1)}), bf16[2,64,1280]{2,1,0:T(8,128)(2,1)S(1)}, u32[]{:S(2)}, u32[]{:S(2)}) async-start(bf16[2,64,1280]{2,1,0:T(8,128)(2,1)} %bitcast), calls=%async_computation | async-start | bytes 655360 | tf_op jit(solution)/shard_map/all_to_all | solution.py:44
  18.0 0.1 copy.40
  18.1 0.1 eq.42
  18.3 0.1 eq.38
  18.5 0.9 reduce-window.6
  19.3 0.2 slice_reduce_fusion
  19.6 0.1 fusion.20
  19.7 0.1 reduce_sum.57
  19.8 0.1 copy.43
  19.9 0.1 convert_bitcast_fusion
  20.0 0.5 copy.39
  20.6 0.2 fusion.11
  20.8 0.2 convert_reduce_fusion
  21.0 0.5 copy-done
  21.5 2.6 convolution_convert_fusion.1
  24.1 2.8 %reshape.76 = bf16[16,36,2560]{2,1,0:T(8,128)(2,1)S(1)} reshape(bf16[576,2560]{1,0:T(8,128)(2,1)} %convolution_convert_fusion.1) | data formatting | bytes 5898240 | tf_op jit(solution)/shard_map/reshape | solution.py:69
  26.9 83.7 %all_to_all.34 = bf16[16,36,2560]{2,1,0:T(8,128)(2,1)} all-to-all(bf16[16,36,2560]{2,1,0:T(8,128)(2,1)S(1)} %reshape.76), channel_id=1, replica_groups=mesh['ep'=16,'dp'=2] {'ep'}, dimensions={0} | all-to-all | bytes 5898240 | tf_op jit(solution)/shard_map/all_to_all | solution.py:68
  110.5 4.5 %reshape.77 = bf16[576,2560]{1,0:T(8,128)(2,1)} reshape(bf16[16,36,2560]{2,1,0:T(8,128)(2,1)} %all_to_all.34) | data formatting | bytes 5898240 | tf_op jit(solution)/shard_map/reshape | solution.py:75
  115.1 13.8 %all-gather.3.cloned.1.call-done = bf16[1152,2560]{1,0:T(8,128)(2,1)} async-done(((bf16[576,2560]{1,0:T(8,128)(2,1)}), bf16[1152,2560]{1,0:T(8,128)(2,1)}) %all-gather.3.cloned.1.call-update) | async-done | bytes 5898256 | tf_op jit(solution)/shard_map/all_gather | solution.py:75
  128.9 8.1 %fusion.2 = f32[1152,768]{1,0:T(8,128)S(1)} fusion(bf16[1152,2560]{1,0:T(8,128)(2,1)} %all-gather.3.cloned.1.call-done, bf16[1,2560,768]{2,1,0:T(8,128)(2,1)} %param.16), kind=kOutput, calls=%fused_computation.5 | convolution fusion | flops 4529848320 | bytes 13369344 | tf_op jit(solution)/shard_map/dot_general | solution.py:76
  137.0 6.1 %fusion.5 = bf16[1152,768]{1,0:T(8,128)(2,1)} fusion(bf16[1152,2560]{1,0:T(8,128)(2,1)S(1)} %copy-done.8, bf16[1,2560,768]{2,1,0:T(8,128)(2,1)S(1)} %copy-done.9, f32[1152,768]{1,0:T(8,128)S(1)} %fusion.2), kind=kOutput, calls=%fused_computation.9 | convolution fusion | flops 4535156736 | bytes 15138816 | tf_op jit(solution)/shard_map/dot_general | solution.py:77
  143.1 14.0 %all-gather.5.cloned.1.call-done = bf16[1152,1536]{1,0:T(8,128)(2,1)} async-done(((bf16[1152,768]{1,0:T(8,128)(2,1)}), bf16[1152,1536]{1,0:T(8,128)(2,1)}) %all-gather.5.cloned.1.call-update) | async-done | bytes 3538960 | tf_op jit(solution)/shard_map/all_gather | solution.py:80
  157.1 7.9 %convolution_convert_fusion = bf16[1152,1280]{1,0:T(8,128)(2,1)S(1)} fusion(bf16[1152,1536]{1,0:T(8,128)(2,1)} %all-gather.5.cloned.1.call-done, bf16[1,1536,1280]{2,1,0:T(8,128)(2,1)} %param.18), kind=kOutput, calls=%fused_computation | convolution fusion | flops 4531322880 | bytes 10420224 | tf_op jit(solution)/shard_map/dot_general | solution.py:79
  165.0 6.1 %all_to_all.35 = bf16[2,576,1280]{2,1,0:T(8,128)(2,1)S(1)} all-to-all(bf16[2,576,1280]{2,1,0:T(8,128)(2,1)S(1)} %bitcast.53), channel_id=1, replica_groups=mesh['ep'=16,'dp'=2] {'dp'}, dimensions={0} | all-to-all | bytes 5898240 | tf_op jit(solution)/shard_map/all_to_all | solution.py:84
  171.1 4.6 %copy.44 = bf16[1,576,2,1280]{3,2,1,0:T(2,128)(2,1)} copy(bf16[1,576,2,1280]{3,1,2,0:T(8,128)(2,1)S(1)} %bitcast.52) | data formatting | bytes 5898240 | tf_op jit(solution)/shard_map/all_to_all | solution.py:84
  175.8 6.4 %reshape.79 = bf16[16,36,2560]{2,1,0:T(8,128)(2,1)S(1)} reshape(bf16[1,576,2,1280]{3,2,1,0:T(2,128)(2,1)} %copy.44) | data formatting | bytes 5898240 | tf_op jit(solution)/shard_map/reshape | solution.py:92
  182.2 82.0 %all_to_all.36 = bf16[16,36,2560]{2,1,0:T(8,128)(2,1)} all-to-all(bf16[16,36,2560]{2,1,0:T(8,128)(2,1)S(1)} %reshape.79), channel_id=1, replica_groups=mesh['ep'=16,'dp'=2] {'ep'}, dimensions={0} | all-to-all | bytes 5898240 | tf_op jit(solution)/shard_map/all_to_all | solution.py:91
  264.2 2.9 %reshape.80 = bf16[576,2560]{1,0:T(8,128)(2,1)S(1)} reshape(bf16[16,36,2560]{2,1,0:T(8,128)(2,1)} %all_to_all.36) | data formatting | bytes 5898240 | tf_op jit(solution)/shard_map/reshape | solution.py:94
  267.1 1.8 fusion.8
  269.0 0.9 fusion.10
  (32 shorter events, 0.3 us)
Async XLA Ops:
  9.7 8.3 %copy-start.4 = (s32[64,6]{0,1:T(8,128)S(1)}, s32[64,6]{0,1:T(8,128)}, u32[]{:S(2)}) copy-start(s32[64,6]{0,1:T(8,128)} %param.14) | copy-start | bytes 4612
  9.7 8.7 %copy-start.5 = (f32[64,6]{0,1:T(8,128)S(1)}, f32[64,6]{0,1:T(8,128)}, u32[]{:S(2)}) copy-start(f32[64,6]{0,1:T(8,128)} %param.15) | copy-start | bytes 4612
  14.4 6.2 %copy-start.3 = (bf16[64,2560]{1,0:T(8,128)(2,1)S(1)}, bf16[64,2560]{1,0:T(8,128)(2,1)}, u32[]{:S(2)}) copy-start(bf16[64,2560]{1,0:T(8,128)(2,1)} %param.11) | copy-start | bytes 983044
  14.4 7.1 %copy-start.6 = (f32[2560]{0:T(1024)S(1)}, f32[2560]{0:T(1024)}, u32[]{:S(2)}) copy-start(f32[2560]{0:T(1024)} %param.13) | copy-start | bytes 30724
  14.4 5.5 %all-to-all-start = ((bf16[2,64,1280]{2,1,0:T(8,128)(2,1)}), bf16[2,64,1280]{2,1,0:T(8,128)(2,1)S(1)}, u32[]{:S(2)}, u32[]{:S(2)}) async-start(bf16[2,64,1280]{2,1,0:T(8,128)(2,1)} %bitcast), calls=%async_computation | async-start | bytes 655360 | tf_op jit(solution)/shard_map/all_to_all | solution.py:44
  18.0 110.9 %all-gather.3.cloned.1.call-start = ((), (), s32[]{:S(2)}) async-start(), calls=%async_computation.4 | async-start | bytes 8847360 | tf_op jit(solution)/shard_map/all_gather | solution.py:75
  20.8 0.7 copy-start
  115.0 42.1 %all-gather.5.cloned.1.call-start = ((), (), s32[]{:S(2)}) async-start(), calls=%async_computation.5 | async-start | bytes 5308416 | tf_op jit(solution)/shard_map/all_gather | solution.py:80
  128.9 8.1 %copy-start.8 = (bf16[1152,2560]{1,0:T(8,128)(2,1)S(1)}, bf16[1152,2560]{1,0:T(8,128)(2,1)}, u32[]{:S(2)}) copy-start(bf16[1152,2560]{1,0:T(8,128)(2,1)} %all-gather.3.cloned.1.call-done) | copy-start | bytes 17694724
  128.9 8.1 %copy-start.9 = (bf16[1,2560,768]{2,1,0:T(8,128)(2,1)S(1)}, bf16[1,2560,768]{2,1,0:T(8,128)(2,1)}, u32[]{:S(2)}) copy-start(bf16[1,2560,768]{2,1,0:T(8,128)(2,1)} %param.17) | copy-start | bytes 11796484
  264.2 3.0 %copy-start.1 = (bf16[64,2560]{1,0:T(8,128)(2,1)S(1)}, bf16[64,2560]{1,0:T(8,128)(2,1)}, u32[]{:S(2)}) copy-start(bf16[64,2560]{1,0:T(8,128)(2,1)} %copy-done) | copy-start | bytes 983044
  264.2 4.8 %copy-start.7 = (f32[2560]{0:T(1024)S(1)}, f32[2560]{0:T(1024)}, u32[]{:S(2)}) copy-start(f32[2560]{0:T(1024)} %param.19) | copy-start | bytes 30724
  269.0 0.9 copy-start.2
Sparse Core Ops, SparseCore 0:
  115.1 13.6 all-gather.2
  143.2 13.8 all-gather.4
where the time goes:
time: 277 us
  blocking collectives  174 us (63%)
  matrix products  31.2 us (11%)
  waiting for transfers between devices  27.8 us (10%)
  local copies, waits for them, and re-layouts  23.1 us (8%)
  between operations  14.2 us (5%)
  starting transfers between devices  3.67 us (1%)
    all_to_all x1, blocking collectives, per_device(): lax.all_to_all(outgoing.reshape(experts, capacity, row_width), 'ep', spli...  83.7 us
    all_to_all x1, blocking collectives, per_device(): lax.all_to_all(joined.reshape(experts, capacity, row_width), 'ep', split_...  82 us
    all_gather x1, waiting for transfers between devices, per_device(): lax.all_gather(hidden, 'dp', axis=1, tiled=True)  14 us
    all_gather x1, waiting for transfers between devices, per_device(): lax.all_gather(arrived.reshape(-1, row_width), 'dp', axis=0, tiled=True)  13.8 us
    dot_general x1, matrix products, per_device(): gate_part = jnp.dot(segment, gate_local, preferred_element_type=jnp.float32)  8.07 us
    dot_general x1, matrix products, per_device(): jnp.dot(lax.all_gather(hidden, 'dp', axis=1, tiled=True), down_local, pre...  7.94 us
    reshape x1, local copies, waits for them, and re-layouts, per_device(): joined.reshape(experts, capacity, row_width)  6.41 us
    all_to_all x1, blocking collectives, per_device(): lax.all_to_all(results.reshape(groups, experts * capacity, part_cols), 'd...  6.1 us
  transfers between devices with their start and end apart: 3, of which 2 were waited for; matrix products, arithmetic and copies ran while one was open for 1% of the time, Pallas kernels for 0%

commit v1 on v0

--- a/solution.py
+++ b/solution.py
@@ -1,6 +1,10 @@
+import functools
+
 import jax
 import jax.numpy as jnp
 from jax import lax
+from jax.experimental import pallas as pl
+from jax.experimental.pallas import tpu as pltpu
 from jax.sharding import PartitionSpec as P
 
 
@@ -13,12 +17,16 @@
 def slot_table(route_block, experts, capacity):
     flat_ids = route_block.reshape(-1)
     onehot = (flat_ids[:, None] == jnp.arange(experts, dtype=jnp.int32)[None, :]).astype(jnp.int32)
-    before = jnp.cumsum(onehot, axis=0) - onehot
+    order = jnp.arange(flat_ids.shape[0], dtype=jnp.int32)
+    earlier = (order[None, :] < order[:, None]).astype(jnp.bfloat16)
+    before = jnp.dot(
+        earlier, onehot.astype(jnp.bfloat16), preferred_element_type=jnp.float32
+    ).astype(jnp.int32)
     rank_in = jnp.sum(before * onehot, axis=1)
     return (flat_ids * capacity + rank_in).reshape(route_block.shape)
 
 
-def per_device(
+def routed_by_collectives(
     attention_out,
     residual,
     out_weight,
@@ -100,9 +108,594 @@
     return (new_state, normed_state)
 
 
+MESH = pl.DeviceIdType.MESH
+NZ = 4
+NP = 4
+IN_PARTS = 5
+OUT_PARTS = 5
+
+
+def remote(src, dst, send, recv, device):
+    return pltpu.make_async_remote_copy(
+        src_ref=src,
+        dst_ref=dst,
+        send_sem=send,
+        recv_sem=recv,
+        device_id=device,
+        device_id_type=MESH,
+    )
+
+
+def fused_kernel(
+    cap,
+    att,
+    res,
+    pre,
+    post,
+    picks,
+    probs,
+    wo_hbm,
+    wg_hbm,
+    wu_hbm,
+    wd_hbm,
+    new_ref,
+    normed_ref,
+    wo,
+    wg,
+    wu,
+    wd,
+    att2,
+    psend,
+    precv,
+    halves,
+    smd,
+    info,
+    icol,
+    comb,
+    place,
+    mix,
+    xcol,
+    stage,
+    xs,
+    acc_g,
+    acc_u,
+    hid,
+    yst,
+    ret,
+    part,
+    chain,
+    dn,
+    up,
+    fsend,
+    frecv,
+    wsem,
+    misc_s,
+    misc_r,
+    info_s,
+    info_r,
+    z_s,
+    z_r,
+    p_s,
+    p_r,
+    f_s,
+    f_r,
+    h_s,
+    h_r,
+    y_s,
+    y_r,
+    dn_s,
+    dn_r,
+    up_s,
+    up_r,
+):
+    f32, bf16 = jnp.float32, jnp.bfloat16
+    ep, c = lax.axis_index("ep"), lax.axis_index("dp")
+    z, mp = ep // NP, ep % NP
+    rows, width = att.shape
+    half = width // 2
+    slots = NZ * cap
+    kw = xcol.shape[2]
+    nw = yst.shape[2]
+    sib = (ep, 1 - c)
+
+    def zdev(other):
+        return (other * NP + mp, c)
+
+    def pdev(other):
+        return (z * NP + other, c)
+
+    def multiple(v, m):
+        return pl.multiple_of(v, m)
+
+    barrier = pltpu.get_barrier_semaphore()
+    pl.semaphore_signal(barrier, inc=1, device_id=sib, device_id_type=MESH)
+    for k in range(1, NZ):
+        pl.semaphore_signal(barrier, inc=1, device_id=zdev((z + k) % NZ), device_id_type=MESH)
+    for k in range(1, NP):
+        pl.semaphore_signal(barrier, inc=1, device_id=pdev((mp + k) % NP), device_id_type=MESH)
+    loads = [
+        pltpu.make_async_copy(wo_hbm, wo, wsem.at[0]),
+        pltpu.make_async_copy(wg_hbm.at[0], wg, wsem.at[1]),
+        pltpu.make_async_copy(wu_hbm.at[0], wu, wsem.at[2]),
+        pltpu.make_async_copy(wd_hbm.at[0], wd, wsem.at[3]),
+    ]
+    for load in loads:
+        load.start()
+    att2[0:rows, :] = att[...]
+    pl.semaphore_wait(barrier, NZ + NP - 1)
+    send_att = remote(
+        att2.at[pl.ds(0, rows)], att2.at[pl.ds(rows, rows)], misc_s.at[0], misc_r.at[0], sib
+    )
+    send_att.start()
+
+    lanes = NZ * rows
+    experts = NZ * NP
+    lane = lax.broadcasted_iota(jnp.int32, (experts, lanes), 1)
+    expert = lax.broadcasted_iota(jnp.int32, (experts, lanes), 0)
+    mine = (lane >= z * rows) & (lane < (z + 1) * rows)
+    prob = probs[...]
+    weight = prob / jnp.sum(prob, axis=0, keepdims=True)
+    chosen = jnp.zeros((experts, lanes), f32)
+    weighted = jnp.zeros((experts, lanes), f32)
+    for k in range(picks.shape[0]):
+        hit = (picks[k : k + 1, :] == expert) & mine
+        chosen = chosen + jnp.where(hit, 1.0, 0.0)
+        weighted = weighted + jnp.where(hit, weight[k : k + 1, :], 0.0)
+    earlier = (
+        lax.broadcasted_iota(jnp.int32, (lanes, lanes), 0)
+        < lax.broadcasted_iota(jnp.int32, (lanes, lanes), 1)
+    )
+    rank = jnp.dot(
+        chosen.astype(bf16), jnp.where(earlier, 1.0, 0.0).astype(bf16), preferred_element_type=f32
+    )
+    offset = (z * cap).astype(f32)
+    target = jnp.where(mine, jnp.where(chosen > 0.5, rank + offset, -1.0), 0.0)
+    for k in range(NZ):
+        info[k, 0:NP, :] = target[k * NP : (k + 1) * NP, :]
+        info[k, NP : 2 * NP, :] = weighted[k * NP : (k + 1) * NP, :]
+    info_sends = []
+    for k in range(1, NZ):
+        other = (z + k) % NZ
+        info_sends.append(
+            remote(info.at[other], icol.at[z], info_s.at[other], info_r.at[z], zdev(other))
+        )
+        info_sends[-1].start()
+    icol[z] = info[z]
+    acc_g[...] = jnp.zeros_like(acc_g)
+    acc_u[...] = jnp.zeros_like(acc_u)
+
+    loads[0].wait()
+    send_att.wait_recv()
+
+    @pl.loop(0, half // 256)
+    def _(n):
+        cols = pl.ds(multiple(n * 256, 256), 256)
+        tile = jnp.dot(att2[...], wo[:, cols], preferred_element_type=f32)
+        halves[c, :, cols] = tile[0:rows]
+        psend[:, cols] = tile[rows:].astype(bf16)
+
+    send_proj = remote(psend, precv, misc_s.at[1], misc_r.at[1], sib)
+    send_proj.start()
+    for k in range(1, NZ):
+        other = (z + k) % NZ
+        remote(
+            info.at[other], icol.at[other], info_s.at[other], info_r.at[other], zdev(other)
+        ).wait_recv()
+    comb[c] = icol[0] + icol[1] + icol[2] + icol[3]
+    send_comb = remote(comb.at[c], comb.at[c], misc_s.at[2], misc_r.at[2], sib)
+    send_comb.start()
+    slot = lax.broadcasted_iota(jnp.int32, (slots, lanes), 0).astype(f32)
+    routed = comb[c]
+    for p in range(NP):
+        place[p * slots : (p + 1) * slots, :] = jnp.where(
+            slot == routed[p : p + 1, :], 1.0, 0.0
+        ).astype(bf16)
+    send_proj.wait_recv()
+    halves[1 - c] = precv[...].astype(f32)
+    squares = jnp.zeros((rows, 1), f32)
+    for h in range(2):
+        summed = (res[:, h * half : (h + 1) * half].astype(f32) + halves[h]).astype(bf16)
+        smd[:, h * half : (h + 1) * half] = summed
+        wide = summed.astype(f32)
+        squares = squares + jnp.sum(wide * wide, axis=1, keepdims=True)
+    scale = lax.rsqrt(squares / width + 1e-06)
+    own = pl.ds(multiple(z * rows, rows), rows)
+    for j in range(IN_PARTS):
+        cols = slice(j * kw, (j + 1) * kw)
+        xcol[j, own, :] = (smd[:, cols].astype(f32) * scale * pre[:, cols]).astype(bf16)
+
+    def zblock(j, b):
+        return xcol.at[j, pl.ds(multiple(b * rows, rows), rows)]
+
+    def zcopy(j, b, d):
+        return remote(
+            zblock(j, b),
+            zblock(j, b),
+            z_s.at[d, j, b],
+            z_r.at[j, b],
+            zdev(jnp.where(d == 0, z + 1, z - 1)),
+        )
+
+    def pick_copy(j, q, device):
+        return remote(
+            stage.at[j, pl.ds(multiple(q * slots, 16), slots)],
+            xs.at[j, pl.ds(multiple(mp * 2 * slots + c * slots, 16), slots)],
+            p_s.at[j, q],
+            p_r.at[j, mp],
+            device,
+        )
+
+    def landed(j, q, core):
+        return xs.at[j, pl.ds(multiple(q * 2 * slots + core * slots, 16), slots)]
+
+    def pass_on(j, q):
+        return remote(landed(j, q, c), landed(j, q, c), f_s.at[j, q], f_r.at[j, q], sib)
+
+    for j in range(IN_PARTS):
+
+        @pl.when(z < NZ - 1)
+        def _():
+            zcopy(j, z, 0).start()
+
+        @pl.when(z > 0)
+        def _():
+            zcopy(j, z, 1).start()
+
+    loads[1].wait()
+    loads[2].wait()
+
+    @pl.loop(0, IN_PARTS + 4)
+    def _(t):
+        for d in range(1, NZ):
+            j = t - (d - 1)
+            ready = (j >= 0) & (j < IN_PARTS)
+
+            @pl.when(ready & (z - d >= 0))
+            def _():
+                zcopy(j, z - d, 0).wait_recv()
+
+                @pl.when(z < NZ - 1)
+                def _():
+                    zcopy(j, z - d, 0).start()
+
+            @pl.when(ready & (z + d < NZ))
+            def _():
+                zcopy(j, z + d, 1).wait_recv()
+
+                @pl.when(z > 0)
+                def _():
+                    zcopy(j, z + d, 1).start()
+
+        j2 = t - 2
+
+        @pl.when((j2 >= 0) & (j2 < IN_PARTS))
+        def _():
+            stage[j2] = jnp.dot(place[...], xcol[j2], preferred_element_type=f32).astype(bf16)
+            for k in range(1, NP):
+                q = (mp + k) % NP
+                pick_copy(j2, q, pdev(q)).start()
+            landed(j2, mp, c)[...] = stage[j2, pl.ds(multiple(mp * slots, 16), slots), :]
+            pass_on(j2, mp).start()
+
+        j3 = t - 3
+
+        @pl.when((j3 >= 0) & (j3 < IN_PARTS))
+        def _():
+            for k in range(1, NP):
+                q = (mp + k) % NP
+                remote(
+                    landed(j3, q, c), landed(j3, q, c), p_s.at[j3, q], p_r.at[j3, q], pdev(q)
+                ).wait_recv()
+                pass_on(j3, q).start()
+
+        j4 = t - 4
+
+        @pl.when((j4 >= 0) & (j4 < IN_PARTS))
+        def _():
+            for q in range(NP):
+                remote(
+                    landed(j4, q, 1 - c), landed(j4, q, 1 - c), f_s.at[j4, q], f_r.at[j4, q], sib
+                ).wait_recv()
+
+            @pl.loop(0, acc_g.shape[1] // 256)
+            def _(n):
+                cols = pl.ds(multiple(n * 256, 256), 256)
+                deep = pl.ds(multiple(j4 * kw, kw), kw)
+                acc_g[:, cols] += jnp.dot(xs[j4], wg[deep, cols], preferred_element_type=f32)
+                acc_u[:, cols] += jnp.dot(xs[j4], wu[deep, cols], preferred_element_type=f32)
+
+    tiles = acc_g.shape[1] // 256
+    for n in range(tiles):
+        cols = slice(n * 256, (n + 1) * 256)
+        gate = acc_g[:, cols]
+        hid[c, n] = (gate / (1.0 + jnp.exp(-gate)) * acc_u[:, cols]).astype(bf16)
+        remote(hid.at[c, n], hid.at[c, n], h_s.at[n], h_r.at[n], sib).start()
+
+    send_comb.wait_send()
+    remote(comb.at[1 - c], comb.at[1 - c], misc_s.at[2], misc_r.at[2], sib).wait_recv()
+    for core in range(2):
+        routed = comb[core]
+        for p in range(NP):
+            spread = jnp.where(slot == routed[p : p + 1, :], routed[NP + p : NP + p + 1, :], 0.0)
+            high = spread.astype(bf16)
+            low = (spread - high.astype(f32)).astype(bf16)
+            mix[core, 0, p * slots : (p + 1) * slots, :] = high
+            mix[core, 1, p * slots : (p + 1) * slots, :] = low
+
+    loads[3].wait()
+    for n in range(tiles):
+        remote(hid.at[1 - c, n], hid.at[1 - c, n], h_s.at[n], h_r.at[n], sib).wait_recv()
+
+    def answer(r, q):
+        return yst.at[r, pl.ds(multiple(q * 2 * slots, 16), 2 * slots)]
+
+    def back(r, q):
+        return remote(answer(r, q), ret.at[r, mp], y_s.at[r, q], y_r.at[r, mp], pdev(q))
+
+    def dn_copy(r, b):
+        return remote(chain.at[r, b], dn.at[r, b], dn_s.at[r, b], dn_r.at[r, b], zdev(z - 1))
+
+    def up_copy(r, b):
+        return remote(chain.at[r, b], up.at[r, b], up_s.at[r, b], up_r.at[r, b], zdev(z + 1))
+
+    @pl.loop(0, OUT_PARTS + 3)
+    def _(t):
+        @pl.when(t < OUT_PARTS)
+        def _():
+            cols = pl.ds(multiple(t * nw, nw), nw)
+            total = jnp.zeros((yst.shape[1], nw), f32)
+            for h in range(2):
+                for n in range(tiles):
+                    first = (h * tiles + n) * 256
+                    total = total + jnp.dot(
+                        hid[h, n], wd[first : first + 256, cols], preferred_element_type=f32
+                    )
+            yst[t] = total.astype(bf16)
+            for k in range(1, NP):
+                q = (mp + k) % NP
+                back(t, q).start()
+            ret[t, mp] = yst[t, pl.ds(multiple(mp * 2 * slots, 16), 2 * slots), :]
+
+        r1 = t - 1
+
+        @pl.when((r1 >= 0) & (r1 < OUT_PARTS))
+        def _():
+            for k in range(1, NP):
+                q = (mp + k) % NP
+                remote(
+                    answer(r1, q), ret.at[r1, q], y_s.at[r1, q], y_r.at[r1, q], pdev(q)
+                ).wait_recv()
+            for core in range(2):
+                total = jnp.zeros((lanes, nw), f32)
+                for p in range(NP):
+                    got = ret[r1, p, core * slots : (core + 1) * slots, :]
+                    for term in range(2):
+                        total = total + lax.dot_general(
+                            mix[core, term, p * slots : (p + 1) * slots, :],
+                            got,
+                            (((0,), (0,)), ((), ())),
+                            preferred_element_type=f32,
+                        )
+                for b in range(NZ):
+                    part[r1, b, core * rows : (core + 1) * rows, :] = total[
+                        b * rows : (b + 1) * rows
+                    ]
+
+        rd = t - 1 - (NZ - 1 - z)
+
+        @pl.when((rd >= 0) & (rd < OUT_PARTS))
+        def _():
+            for b in range(NZ - 1):
+
+                @pl.when((b < z) & (z == NZ - 1))
+                def _():
+                    chain[rd, b] = part[rd, b].astype(bf16)
+                    dn_copy(rd, b).start()
+
+                @pl.when((b < z) & (z < NZ - 1))
+                def _():
+                    dn_copy(rd, b).wait_recv()
+                    chain[rd, b] = (part[rd, b] + dn[rd, b].astype(f32)).astype(bf16)
+                    dn_copy(rd, b).start()
+
+        ru = t - 1 - z
+
+        @pl.when((ru >= 0) & (ru < OUT_PARTS))
+        def _():
+            for b in range(1, NZ):
+
+                @pl.when((b > z) & (z == 0))
+                def _():
+                    chain[ru, b] = part[ru, b].astype(bf16)
+                    up_copy(ru, b).start()
+
+                @pl.when((b > z) & (z > 0))
+                def _():
+                    up_copy(ru, b).wait_recv()
+                    chain[ru, b] = (part[ru, b] + up[ru, b].astype(f32)).astype(bf16)
+                    up_copy(ru, b).start()
+
+    for r in range(OUT_PARTS):
+        cols = slice(r * nw, (r + 1) * nw)
+
+        @pl.when(z < NZ - 1)
+        def _():
+            dn_copy(r, z).wait_recv()
+            part[r, z] = part[r, z] + dn[r, z].astype(f32)
+
+        @pl.when(z > 0)
+        def _():
+            up_copy(r, z).wait_recv()
+            part[r, z] = part[r, z] + up[r, z].astype(f32)
+
+        halves[c, :, cols] = part[r, z, pl.ds(multiple(c * rows, rows), rows), :]
+        fsend[:, cols] = part[r, z, pl.ds(multiple((1 - c) * rows, rows), rows), :]
+    send_last = remote(fsend, frecv, misc_s.at[3], misc_r.at[3], sib)
+    send_last.start()
+    send_last.wait_recv()
+    halves[1 - c] = frecv[...]
+    squares = jnp.zeros((rows, 1), f32)
+    for h in range(2):
+        cols = slice(h * half, (h + 1) * half)
+        state = (smd[:, cols].astype(f32) + halves[h]).astype(bf16)
+        new_ref[:, cols] = state
+        wide = state.astype(f32)
+        squares = squares + jnp.sum(wide * wide, axis=1, keepdims=True)
+    scale = lax.rsqrt(squares / width + 1e-06)
+    for h in range(2):
+        cols = slice(h * half, (h + 1) * half)
+        normed_ref[:, cols] = (new_ref[:, cols].astype(f32) * scale * post[:, cols]).astype(bf16)
+
+    send_att.wait_send()
+    send_proj.wait_send()
+    send_last.wait_send()
+    for copy in info_sends:
+        copy.wait_send()
+    for n in range(tiles):
+        remote(hid.at[c, n], hid.at[c, n], h_s.at[n], h_r.at[n], sib).wait_send()
+
+    @pl.loop(0, IN_PARTS)
+    def _(j):
+        for b in range(NZ):
+
+            @pl.when((z < NZ - 1) & (b <= z))
+            def _():
+                zcopy(j, b, 0).wait_send()
+
+            @pl.when((z > 0) & (b >= z))
+            def _():
+                zcopy(j, b, 1).wait_send()
+
+        for k in range(1, NP):
+            q = (mp + k) % NP
+            pick_copy(j, q, pdev(q)).wait_send()
+        for q in range(NP):
+            pass_on(j, q).wait_send()
+
+    @pl.loop(0, OUT_PARTS)
+    def _(r):
+        for k in range(1, NP):
+            q = (mp + k) % NP
+            back(r, q).wait_send()
+        for b in range(NZ):
+
+            @pl.when(b < z)
+            def _():
+                dn_copy(r, b).wait_send()
+
+            @pl.when(b > z)
+            def _():
+                up_copy(r, b).wait_send()
+
+
+def fused(
+    attention_out,
+    residual,
+    out_weight,
+    pre_gain,
+    routes,
+    gate_prob,
+    gate_weight,
+    up_weight,
+    down_weight,
+    post_gain,
+):
+    rows, width = residual.shape
+    top = routes.shape[1]
+    half = width // 2
+    hidden = gate_weight.shape[2]
+    cap = max(2, 3 * rows * top // (2 * NZ * NP))
+    slots = NZ * cap
+    lanes = NZ * rows
+    total = 2 * NP * slots
+    kw, nw = width // IN_PARTS, half // OUT_PARTS
+    f32, bf16 = jnp.float32, jnp.bfloat16
+    dma = pltpu.SemaphoreType.DMA
+    vmem = pl.BlockSpec(memory_space=pltpu.VMEM)
+    hbm = pl.BlockSpec(memory_space=pl.ANY)
+    return pl.pallas_call(
+        functools.partial(fused_kernel, cap),
+        out_shape=(
+            jax.ShapeDtypeStruct((rows, width), bf16),
+            jax.ShapeDtypeStruct((rows, width), bf16),
+        ),
+        in_specs=[vmem] * 6 + [hbm] * 4,
+        out_specs=(vmem, vmem),
+        scratch_shapes=[
+            pltpu.VMEM((width, half), bf16),
+            pltpu.VMEM((width, hidden), bf16),
+            pltpu.VMEM((width, hidden), bf16),
+            pltpu.VMEM((2 * hidden, half), bf16),
+            pltpu.VMEM((2 * rows, width), bf16),
+            pltpu.VMEM((rows, half), bf16),
+            pltpu.VMEM((rows, half), bf16),
+            pltpu.VMEM((2, rows, half), f32),
+            pltpu.VMEM((rows, width), bf16),
+            pltpu.VMEM((NZ, 2 * NP, lanes), f32),
+            pltpu.VMEM((NZ, 2 * NP, lanes), f32),
+            pltpu.VMEM((2, 2 * NP, lanes), f32),
+            pltpu.VMEM((NP * slots, lanes), bf16),
+            pltpu.VMEM((2, 2, NP * slots, lanes), bf16),
+            pltpu.VMEM((IN_PARTS, lanes, kw), bf16),
+            pltpu.VMEM((IN_PARTS, NP * slots, kw), bf16),
+            pltpu.VMEM((IN_PARTS, total, kw), bf16),
+            pltpu.VMEM((total, hidden), f32),
+            pltpu.VMEM((total, hidden), f32),
+            pltpu.VMEM((2, hidden // 256, total, 256), bf16),
+            pltpu.VMEM((OUT_PARTS, total, nw), bf16),
+            pltpu.VMEM((OUT_PARTS, NP, 2 * slots, nw), bf16),
+            pltpu.VMEM((OUT_PARTS, NZ, 2 * rows, nw), f32),
+            pltpu.VMEM((OUT_PARTS, NZ, 2 * rows, nw), bf16),
+            pltpu.VMEM((OUT_PARTS, NZ, 2 * rows, nw), bf16),
+            pltpu.VMEM((OUT_PARTS, NZ, 2 * rows, nw), bf16),
+            pltpu.VMEM((rows, half), f32),
+            pltpu.VMEM((rows, half), f32),
+            dma((4,)),
+            dma((4,)),
+            dma((4,)),
+            dma((NZ,)),
+            dma((NZ,)),
+            dma((2, IN_PARTS, NZ)),
+            dma((IN_PARTS, NZ)),
+            dma((IN_PARTS, NP)),
+            dma((IN_PARTS, NP)),
+            dma((IN_PARTS, NP)),
+            dma((IN_PARTS, NP)),
+            dma((hidden // 256,)),
+            dma((hidden // 256,)),
+            dma((OUT_PARTS, NP)),
+            dma((OUT_PARTS, NP)),
+            dma((OUT_PARTS, NZ)),
+            dma((OUT_PARTS, NZ)),
+            dma((OUT_PARTS, NZ)),
+            dma((OUT_PARTS, NZ)),
+        ],
+        compiler_params=pltpu.CompilerParams(
+            collective_id=0, has_side_effects=True, vmem_limit_bytes=62 * 1024 * 1024
+        ),
+    )(
+        attention_out,
+        residual,
+        pre_gain.reshape(1, width),
+        post_gain.reshape(1, width),
+        jnp.tile(routes.T, (1, NZ)),
+        jnp.tile(gate_prob.T, (1, NZ)),
+        out_weight,
+        gate_weight,
+        up_weight,
+        down_weight,
+    )
+
+
+def per_device(chips, *arrays):
+    if chips == NZ * NP:
+        return fused(*arrays)
+    return routed_by_collectives(*arrays)
+
+
 def solution(mesh):
     return jax.shard_map(
-        per_device,
+        functools.partial(per_device, mesh.shape["ep"]),
         mesh=mesh,
         in_specs=(
             P(("ep", "dp"), None),

time: 277 us -> 127 us (0.46)
  blocking collectives: 174 us -> 0 us
  Pallas kernels: 0 us -> 117 us
  matrix products: 31.2 us -> 0 us
  waiting for transfers between devices: 27.8 us -> 0 us
  local copies, waits for them, and re-layouts: 23.1 us -> 8.79 us
  between operations: 14.2 us -> 0.64 us
  starting transfers between devices: 3.67 us -> 0 us
    all_to_all x3 -> x0, blocking collectives: 172 us -> none  [the longest x1 83.7 us: per_device(): lax.all_to_all(outgoing.reshape(experts, capacity, row_width), 'ep', spli...]
    pallas_call x0 -> x1, Pallas kernels: none -> 117 us  [fused(): pl.pallas_call(functools.partial(fused_kernel, cap), out_shape=(jax.Shape...]
    dot_general x6 -> x0, matrix products: 31.2 us -> none  [the longest x1 8.07 us: per_device(): gate_part = jnp.dot(segment, gate_local, preferred_element_type=jnp.float32)]
    all_gather x2 -> x0, waiting for transfers between devices: 27.8 us -> none  [the longest x1 14 us: per_device(): lax.all_gather(hidden, 'dp', axis=1, tiled=True)]
    reshape x4 -> x2, local copies, waits for them, and re-layouts: 16.6 us -> 2.63 us  [the longest x1 1.31 us: fused(): pre_gain.reshape(1, width)]
    all_to_all x1 -> x0, local copies, waits for them, and re-layouts: 4.63 us -> none  [per_device(): lax.all_to_all(results.reshape(groups, experts * capacity, part_cols), 'd...]
    all_to_all x1 -> x0, starting transfers between devices: 3.59 us -> none  [per_device(): lax.all_to_all(columns.reshape(groups, tok_rows, part_cols).astype(jnp.bf...]
    unnamed x22 -> x2, local copies, waits for them, and re-layouts: 0.63 us -> 3.44 us
  transfers between devices with their start and end apart: 3 -> 0, of which waited for: 2 -> 0; matrix products, arithmetic and copies ran while one was open for 1% -> 0% of each run, Pallas kernels for 0% -> 0%
where the time goes in v1:
time: 127 us; the launch traced here: 126 us
  Pallas kernels  117 us (92%)
  local copies, waits for them, and re-layouts  8.79 us (7%)
    pallas_call x1, Pallas kernels, fused(): pl.pallas_call(functools.partial(fused_kernel, cap), out_shape=(jax.Shape...  117 us
    unnamed x2, local copies, waits for them, and re-layouts  3.44 us

profile of v1, /device:TPU:0, one launch (start us, length us, event | category | flops | bytes accessed | tf_op | source)
XLA Modules:
  0.0 126.2 jit_solution(7923907790620087806)
XLA Ops:
  0.6 1.3 %reshape.18.pre = f32[1,2560]{1,0:T(1,128)} reshape(f32[2560]{0:T(1024)} %param.13) | data formatting | bytes 20480 | tf_op jit(solution)/shard_map/reshape | solution.py:679
  1.9 1.3 %reshape.19.post = f32[1,2560]{1,0:T(1,128)} reshape(f32[2560]{0:T(1024)} %param.19) | data formatting | bytes 20480 | tf_op jit(solution)/shard_map/reshape | solution.py:680
  3.3 0.7 tile.8
  3.9 0.7 tile.9.picks
  4.6 0.7 tile.20
  5.3 0.7 tile.21.probs
  6.0 116.7 %shard_map.113 = (bf16[64,2560]{1,0:T(8,128)(2,1)}, bf16[64,2560]{1,0:T(8,128)(2,1)}) custom-call(bf16[64,2560]{1,0:T(8,128)(2,1)} %att.1, bf16[64,2560]{1,0:T(8,128)(2,1)} %res.1, f32[1,2560]{1,0:T(1,128)} %reshape.18.pre, f32[1,2560]{1,0:T(1,128)} %reshape.19.post, s32[6,256]{1,0:T(8,128)} %tile.9.picks, f32[6,256]{1,0:T(8,128)} %tile.21.probs, ...), custom_call_target="tpu_custom_call" | custom-call | tf_op jit(solution)/shard_map/pallas_call | solution.py:616
  122.7 1.7 %copy.14 = bf16[64,2560]{1,0:T(8,128)(2,1)} copy(bf16[64,2560]{1,0:T(8,128)(2,1)} %get-tuple-element.4) | data formatting | bytes 655360
  124.5 1.7 %copy.15 = bf16[64,2560]{1,0:T(8,128)(2,1)} copy(bf16[64,2560]{1,0:T(8,128)(2,1)} %get-tuple-element.5) | data formatting | bytes 655360

commit v2 on v1

--- a/solution.py
+++ b/solution.py
@@ -112,6 +112,7 @@
 NZ = 4
 NP = 4
 IN_PARTS = 5
+AHEAD = 2
 OUT_PARTS = 5
 
 
@@ -128,18 +129,21 @@
 
 def fused_kernel(
     cap,
-    att,
-    res,
-    pre,
-    post,
-    picks,
-    probs,
+    att_hbm,
+    res_hbm,
+    pre_hbm,
+    picks_hbm,
+    probs_hbm,
     wo_hbm,
     wg_hbm,
     wu_hbm,
     wd_hbm,
-    new_ref,
-    normed_ref,
+    sum_ref,
+    expert_ref,
+    res,
+    pre,
+    picks,
+    probs,
     wo,
     wg,
     wu,
@@ -187,11 +191,15 @@
     dn_r,
     up_s,
     up_r,
+    proj_s,
+    proj_r,
+    last_s,
+    last_r,
 ):
     f32, bf16 = jnp.float32, jnp.bfloat16
     ep, c = lax.axis_index("ep"), lax.axis_index("dp")
     z, mp = ep // NP, ep % NP
-    rows, width = att.shape
+    rows, width = res.shape
     half = width // 2
     slots = NZ * cap
     kw = xcol.shape[2]
@@ -219,9 +227,16 @@
         pltpu.make_async_copy(wu_hbm.at[0], wu, wsem.at[2]),
         pltpu.make_async_copy(wd_hbm.at[0], wd, wsem.at[3]),
     ]
-    for load in loads:
+    small = [
+        pltpu.make_async_copy(att_hbm, att2.at[pl.ds(0, rows)], wsem.at[4]),
+        pltpu.make_async_copy(picks_hbm, picks, wsem.at[5]),
+        pltpu.make_async_copy(probs_hbm, probs, wsem.at[6]),
+        pltpu.make_async_copy(res_hbm, res, wsem.at[7]),
+        pltpu.make_async_copy(pre_hbm, pre.at[0], wsem.at[8]),
+    ]
+    for load in small[0:3] + loads[0:1] + small[3:]:
         load.start()
-    att2[0:rows, :] = att[...]
+    small[0].wait()
     pl.semaphore_wait(barrier, NZ + NP - 1)
     send_att = remote(
         att2.at[pl.ds(0, rows)], att2.at[pl.ds(rows, rows)], misc_s.at[0], misc_r.at[0], sib
@@ -233,12 +248,28 @@
     lane = lax.broadcasted_iota(jnp.int32, (experts, lanes), 1)
     expert = lax.broadcasted_iota(jnp.int32, (experts, lanes), 0)
     mine = (lane >= z * rows) & (lane < (z + 1) * rows)
+    small[1].wait()
+    small[2].wait()
+    spot = jnp.where(
+        lax.broadcasted_iota(jnp.int32, (rows, lanes), 0) + z * rows
+        == lax.broadcasted_iota(jnp.int32, (rows, lanes), 1),
+        1.0,
+        0.0,
+    ).astype(bf16)
+
+    def spread_out(values):
+        return jnp.dot(values.astype(bf16), spot, preferred_element_type=f32)
+
+    named = spread_out(picks[...].astype(f32)).astype(jnp.int32)
     prob = probs[...]
-    weight = prob / jnp.sum(prob, axis=0, keepdims=True)
+    share = prob / jnp.sum(prob, axis=0, keepdims=True)
+    term1 = share.astype(bf16).astype(f32)
+    term2 = (share - term1).astype(bf16).astype(f32)
+    weight = spread_out(term1) + spread_out(term2) + spread_out(share - term1 - term2)
     chosen = jnp.zeros((experts, lanes), f32)
     weighted = jnp.zeros((experts, lanes), f32)
     for k in range(picks.shape[0]):
-        hit = (picks[k : k + 1, :] == expert) & mine
+        hit = (named[k : k + 1, :] == expert) & mine
         chosen = chosen + jnp.where(hit, 1.0, 0.0)
         weighted = weighted + jnp.where(hit, weight[k : k + 1, :], 0.0)
     earlier = (
@@ -261,21 +292,20 @@
         )
         info_sends[-1].start()
     icol[z] = info[z]
-    acc_g[...] = jnp.zeros_like(acc_g)
-    acc_u[...] = jnp.zeros_like(acc_u)
 
     loads[0].wait()
+    for load in loads[1:]:
+        load.start()
     send_att.wait_recv()
 
-    @pl.loop(0, half // 256)
-    def _(n):
-        cols = pl.ds(multiple(n * 256, 256), 256)
+    send_proj = []
+    for n in range(half // 256):
+        cols = slice(n * 256, (n + 1) * 256)
         tile = jnp.dot(att2[...], wo[:, cols], preferred_element_type=f32)
         halves[c, :, cols] = tile[0:rows]
-        psend[:, cols] = tile[rows:].astype(bf16)
-
-    send_proj = remote(psend, precv, misc_s.at[1], misc_r.at[1], sib)
-    send_proj.start()
+        psend[n] = tile[rows:].astype(bf16)
+        send_proj.append(remote(psend.at[n], precv.at[n], proj_s.at[n], proj_r.at[n], sib))
+        send_proj[n].start()
     for k in range(1, NZ):
         other = (z + k) % NZ
         remote(
@@ -290,8 +320,11 @@
         place[p * slots : (p + 1) * slots, :] = jnp.where(
             slot == routed[p : p + 1, :], 1.0, 0.0
         ).astype(bf16)
-    send_proj.wait_recv()
-    halves[1 - c] = precv[...].astype(f32)
+    for load in small[3:]:
+        load.wait()
+    for n in range(half // 256):
+        send_proj[n].wait_recv()
+        halves[1 - c, :, n * 256 : (n + 1) * 256] = precv[n].astype(f32)
     squares = jnp.zeros((rows, 1), f32)
     for h in range(2):
         summed = (res[:, h * half : (h + 1) * half].astype(f32) + halves[h]).astype(bf16)
@@ -300,9 +333,6 @@
         squares = squares + jnp.sum(wide * wide, axis=1, keepdims=True)
     scale = lax.rsqrt(squares / width + 1e-06)
     own = pl.ds(multiple(z * rows, rows), rows)
-    for j in range(IN_PARTS):
-        cols = slice(j * kw, (j + 1) * kw)
-        xcol[j, own, :] = (smd[:, cols].astype(f32) * scale * pre[:, cols]).astype(bf16)
 
     def zblock(j, b):
         return xcol.at[j, pl.ds(multiple(b * rows, rows), rows)]
@@ -331,16 +361,22 @@
     def pass_on(j, q):
         return remote(landed(j, q, c), landed(j, q, c), f_s.at[j, q], f_r.at[j, q], sib)
 
+    def send_own(j):
+        @pl.when(z < NZ - 1)
+        def _():
+            zcopy(j, z, 0).start()
+
+        @pl.when(z > 0)
+        def _():
+            zcopy(j, z, 1).start()
+
     for j in range(IN_PARTS):
-
-        @pl.when(z < NZ - 1)
-        def _():
-            zcopy(j, z, 0).start()
-
-        @pl.when(z > 0)
-        def _():
-            zcopy(j, z, 1).start()
-
+        cols = slice(j * kw, (j + 1) * kw)
+        xcol[j, own, :] = (smd[:, cols].astype(f32) * scale * pre[:, cols]).astype(bf16)
+        if j < AHEAD:
+            send_own(j)
+    acc_g[...] = jnp.zeros_like(acc_g)
+    acc_u[...] = jnp.zeros_like(acc_u)
     loads[1].wait()
     loads[2].wait()
 
@@ -365,6 +401,10 @@
                 @pl.when(z > 0)
                 def _():
                     zcopy(j, z + d, 1).start()
+
+        @pl.when(t + AHEAD < IN_PARTS)
+        def _():
+            send_own(t + AHEAD)
 
         j2 = t - 2
 
@@ -437,6 +477,8 @@
 
     def up_copy(r, b):
         return remote(chain.at[r, b], up.at[r, b], up_s.at[r, b], up_r.at[r, b], zdev(z + 1))
+
+    send_last = []
 
     @pl.loop(0, OUT_PARTS + 3)
     def _(t):
@@ -529,26 +571,18 @@
             part[r, z] = part[r, z] + up[r, z].astype(f32)
 
         halves[c, :, cols] = part[r, z, pl.ds(multiple(c * rows, rows), rows), :]
-        fsend[:, cols] = part[r, z, pl.ds(multiple((1 - c) * rows, rows), rows), :]
-    send_last = remote(fsend, frecv, misc_s.at[3], misc_r.at[3], sib)
-    send_last.start()
-    send_last.wait_recv()
-    halves[1 - c] = frecv[...]
-    squares = jnp.zeros((rows, 1), f32)
-    for h in range(2):
-        cols = slice(h * half, (h + 1) * half)
-        state = (smd[:, cols].astype(f32) + halves[h]).astype(bf16)
-        new_ref[:, cols] = state
-        wide = state.astype(f32)
-        squares = squares + jnp.sum(wide * wide, axis=1, keepdims=True)
-    scale = lax.rsqrt(squares / width + 1e-06)
-    for h in range(2):
-        cols = slice(h * half, (h + 1) * half)
-        normed_ref[:, cols] = (new_ref[:, cols].astype(f32) * scale * post[:, cols]).astype(bf16)
+        fsend[r] = part[r, z, pl.ds(multiple((1 - c) * rows, rows), rows), :]
+        send_last.append(remote(fsend.at[r], frecv.at[r], last_s.at[r], last_r.at[r], sib))
+        send_last[r].start()
+    for r in range(OUT_PARTS):
+        send_last[r].wait_recv()
+        halves[1 - c, :, r * nw : (r + 1) * nw] = frecv[r]
+    sum_ref[...] = smd[...]
+    expert_ref[...] = halves[...]
 
     send_att.wait_send()
-    send_proj.wait_send()
-    send_last.wait_send()
+    for copy in send_proj + send_last:
+        copy.wait_send()
     for copy in info_sends:
         copy.wait_send()
     for n in range(tiles):
@@ -586,6 +620,26 @@
             @pl.when(b > z)
             def _():
                 up_copy(r, b).wait_send()
+
+
+def end_kernel(sum_ref, expert_ref, post_hbm, new_ref, normed_ref, post, sem):
+    f32, bf16 = jnp.float32, jnp.bfloat16
+    load = pltpu.make_async_copy(post_hbm, post.at[0], sem)
+    load.start()
+    rows, width = sum_ref.shape
+    half = width // 2
+    squares = jnp.zeros((rows, 1), f32)
+    for h in range(2):
+        cols = slice(h * half, (h + 1) * half)
+        state = (sum_ref[:, cols].astype(f32) + expert_ref[h]).astype(bf16)
+        new_ref[:, cols] = state
+        wide = state.astype(f32)
+        squares = squares + jnp.sum(wide * wide, axis=1, keepdims=True)
+    scale = lax.rsqrt(squares / width + 1e-06)
+    load.wait()
+    for h in range(2):
+        cols = slice(h * half, (h + 1) * half)
+        normed_ref[:, cols] = (new_ref[:, cols].astype(f32) * scale * post[:, cols]).astype(bf16)
 
 
 def fused(
@@ -613,22 +667,26 @@
     dma = pltpu.SemaphoreType.DMA
     vmem = pl.BlockSpec(memory_space=pltpu.VMEM)
     hbm = pl.BlockSpec(memory_space=pl.ANY)
-    return pl.pallas_call(
+    summed, expert_sum = pl.pallas_call(
         functools.partial(fused_kernel, cap),
         out_shape=(
             jax.ShapeDtypeStruct((rows, width), bf16),
-            jax.ShapeDtypeStruct((rows, width), bf16),
+            jax.ShapeDtypeStruct((2, rows, half), f32),
         ),
-        in_specs=[vmem] * 6 + [hbm] * 4,
+        in_specs=[hbm] * 9,
         out_specs=(vmem, vmem),
         scratch_shapes=[
+            pltpu.VMEM((rows, width), bf16),
+            pltpu.VMEM((1, width), f32),
+            pltpu.VMEM((top, rows), jnp.int32),
+            pltpu.VMEM((top, rows), f32),
             pltpu.VMEM((width, half), bf16),
             pltpu.VMEM((width, hidden), bf16),
             pltpu.VMEM((width, hidden), bf16),
             pltpu.VMEM((2 * hidden, half), bf16),
             pltpu.VMEM((2 * rows, width), bf16),
-            pltpu.VMEM((rows, half), bf16),
-            pltpu.VMEM((rows, half), bf16),
+            pltpu.VMEM((half // 256, rows, 256), bf16),
+            pltpu.VMEM((half // 256, rows, 256), bf16),
             pltpu.VMEM((2, rows, half), f32),
             pltpu.VMEM((rows, width), bf16),
             pltpu.VMEM((NZ, 2 * NP, lanes), f32),
@@ -648,9 +706,9 @@
             pltpu.VMEM((OUT_PARTS, NZ, 2 * rows, nw), bf16),
             pltpu.VMEM((OUT_PARTS, NZ, 2 * rows, nw), bf16),
             pltpu.VMEM((OUT_PARTS, NZ, 2 * rows, nw), bf16),
-            pltpu.VMEM((rows, half), f32),
-            pltpu.VMEM((rows, half), f32),
-            dma((4,)),
+            pltpu.VMEM((OUT_PARTS, rows, nw), f32),
+            pltpu.VMEM((OUT_PARTS, rows, nw), f32),
+            dma((10,)),
             dma((4,)),
             dma((4,)),
             dma((NZ,)),
@@ -669,6 +727,10 @@
             dma((OUT_PARTS, NZ)),
             dma((OUT_PARTS, NZ)),
             dma((OUT_PARTS, NZ)),
+            dma((half // 256,)),
+            dma((half // 256,)),
+            dma((OUT_PARTS,)),
+            dma((OUT_PARTS,)),
         ],
         compiler_params=pltpu.CompilerParams(
             collective_id=0, has_side_effects=True, vmem_limit_bytes=62 * 1024 * 1024
@@ -676,15 +738,24 @@
     )(
         attention_out,
         residual,
-        pre_gain.reshape(1, width),
-        post_gain.reshape(1, width),
-        jnp.tile(routes.T, (1, NZ)),
-        jnp.tile(gate_prob.T, (1, NZ)),
+        pre_gain,
+        routes.T,
+        gate_prob.T,
         out_weight,
         gate_weight,
         up_weight,
         down_weight,
     )
+    return pl.pallas_call(
+        end_kernel,
+        out_shape=(
+            jax.ShapeDtypeStruct((rows, width), bf16),
+            jax.ShapeDtypeStruct((rows, width), bf16),
+        ),
+        in_specs=[vmem, vmem, hbm],
+        out_specs=(vmem, vmem),
+        scratch_shapes=[pltpu.VMEM((1, width), f32), dma(())],
+    )(summed, expert_sum, post_gain)
 
 
 def per_device(chips, *arrays):

time: 127 us -> 117 us (0.921)
  local copies, waits for them, and re-layouts: 8.79 us -> 0 us
    pallas_call x1, Pallas kernels: 117 us -> 113 us  [fused(): pl.pallas_call(functools.partial(fused_kernel, cap), out_shape=(jax.Shape...]
    unnamed x2 -> x0, local copies, waits for them, and re-layouts: 3.44 us -> none
    pallas_call x0 -> x1, Pallas kernels: none -> 2.74 us  [fused(): pl.pallas_call(end_kernel, out_shape=(jax.ShapeDtypeStruct((rows, width),...]
    another operation x4 -> x0, local copies, waits for them, and re-layouts: 2.73 us -> none  [the longest x2 1.36 us: fused(): jnp.tile(routes.T, (1, NZ))]
    reshape x2 -> x0, local copies, waits for them, and re-layouts: 2.63 us -> none  [the longest x1 1.31 us: fused(): pre_gain.reshape(1, width)]
where the time goes in v2:
time: 117 us; the launch traced here: 116 us
  Pallas kernels  116 us (99%)
    pallas_call x1, Pallas kernels, fused(): pl.pallas_call(functools.partial(fused_kernel, cap), out_shape=(jax.Shape...  113 us
    pallas_call x1, Pallas kernels, fused(): pl.pallas_call(end_kernel, out_shape=(jax.ShapeDtypeStruct((rows, width),...  2.74 us

profile of v2, /device:TPU:0, one launch (start us, length us, event | category | flops | bytes accessed | tf_op | source)
XLA Modules:
  0.0 116.3 jit_solution(9580637184588242051)
XLA Ops:
  0.6 112.9 %shard_map.113 = (bf16[64,2560]{1,0:T(8,128)(2,1)}, f32[2,64,1280]{2,1,0:T(8,128)}) custom-call(bf16[64,2560]{1,0:T(8,128)(2,1)} %att_hbm.1, bf16[64,2560]{1,0:T(8,128)(2,1)} %res_hbm.1, f32[2560]{0:T(1024)} %pre_hbm.1, s32[6,64]{1,0:T(8,128)} %bitcast.2, f32[6,64]{1,0:T(8,128)} %bitcast.3, bf16[2560,1280]{1,0:T(8,128)(2,1)} %wo_hbm.1, ...), custom_call_target="tpu_custom_call" | custom-call | tf_op jit(solution)/shard_map/pallas_call | solution.py:670
  113.5 2.7 %shard_map.114 = (bf16[64,2560]{1,0:T(8,128)(2,1)}, bf16[64,2560]{1,0:T(8,128)(2,1)}) custom-call(bf16[64,2560]{1,0:T(8,128)(2,1)} %get-tuple-element.4.sum_ref, f32[2,64,1280]{2,1,0:T(8,128)} %get-tuple-element.5.expert_ref, f32[2560]{0:T(1024)} %post_hbm.1), custom_call_target="tpu_custom_call" | custom-call | tf_op jit(solution)/shard_map/pallas_call | solution.py:749
